TPU v7x, 256 devices: a whole 4x4x8 slice. The times are simulated.
256 devices in a mesh: dp: 16 (over z_hi, y, core), space: 16 (over x, z_lo).
Axes of the slice: x: 4, y: 4, z: 8 (z_hi: 2, z_lo: 4; z = z_hi * 4 + z_lo), core: 2. Of those that a mesh axis runs over, the one named last changes fastest.
Arguments:
- state: bfloat16 [16, 5, 256, 96, 192], P('dp', None, 'space'), may hold values from -6 to 6
- cotangent: bfloat16 [16, 5, 256, 96, 192], P('dp', None, 'space'), may hold values from -24 to 24
- x_operator: bfloat16 [256, 256], replicated, may hold values from -0.375 to 0.375
- y_operator: bfloat16 [96, 96], replicated, may hold values from -0.625 to 0.625
- z_operator: bfloat16 [192, 192], replicated, may hold values from -0.4375 to 0.4375
- w_in: bfloat16 [64, 20], replicated, may hold values from -1.25 to 1.25
- b_in: float32 [64], replicated, may hold values from -3 to 3
- w_out: bfloat16 [5, 64], replicated, may hold values from -0.75 to 0.75
- b_out: float32 [5], replicated, may hold values from -3 to 3
Outputs:
- new_state: bfloat16 [16, 5, 256, 96, 192], P('dp', None, 'space')
- state_grad: bfloat16 [16, 5, 256, 96, 192], P('dp', None, 'space')
- w_in_grad: float32 [64, 20], replicated
- b_in_grad: float32 [64], replicated
- w_out_grad: float32 [5, 64], replicated
- b_out_grad: float32 [5], replicated
All inputs are finite; a program needn't handle non-finite values.
Results may differ from a plain program's by a relative error of at most 0.012.
Values may be sent and summed in bfloat16 or wider, within the bound.
A program may use at most 128 MiB of HBM per device.

v0:
```python
import math

import jax
import jax.numpy as jnp
from jax import lax
from jax.sharding import PartitionSpec as P

STEP_SIZE = 0.5


def row_work(state_row, grad_xb, grad_yb, grad_zb, cot_row, w_in, b_in, w_out, b_out):
    fields = state_row.shape[0]
    cells = state_row.shape[1]
    features = jnp.concatenate([state_row, grad_xb, grad_yb, grad_zb], axis=0)
    before = jnp.dot(w_in, features, preferred_element_type=jnp.float32) + b_in[:, None]
    active = jnp.tanh(before)
    hidden = active.astype(jnp.bfloat16)
    closure = jnp.dot(w_out, hidden, preferred_element_type=jnp.float32) + b_out[:, None]
    state_f = state_row.astype(jnp.float32)
    grad_xf = grad_xb.astype(jnp.float32)
    grad_yf = grad_yb.astype(jnp.float32)
    grad_zf = grad_zb.astype(jnp.float32)
    vel_x = state_f[0:1]
    vel_y = state_f[1:2]
    vel_z = state_f[2:3]
    advect = vel_x * grad_xf + vel_y * grad_yf + vel_z * grad_zf
    updated = (state_f + STEP_SIZE * (closure - advect)).astype(jnp.bfloat16)
    cot_f = cot_row.astype(jnp.float32)
    d_closure = (STEP_SIZE * cot_f).astype(jnp.bfloat16)
    w_out_part = jnp.dot(d_closure, hidden.T, preferred_element_type=jnp.float32)
    b_out_part = jnp.sum(d_closure.astype(jnp.float32), axis=1)
    d_hidden = jnp.dot(w_out.T, d_closure, preferred_element_type=jnp.float32)
    d_before = (d_hidden * (1.0 - active * active)).astype(jnp.bfloat16)
    w_in_part = jnp.dot(d_before, features.T, preferred_element_type=jnp.float32)
    b_in_part = jnp.sum(d_before.astype(jnp.float32), axis=1)
    d_features = jnp.dot(w_in.T, d_before, preferred_element_type=jnp.float32)
    d_advect = -STEP_SIZE * cot_f
    cot_x = (d_features[fields : 2 * fields] + d_advect * vel_x).astype(jnp.bfloat16)
    cot_y = (d_features[2 * fields : 3 * fields] + d_advect * vel_y).astype(jnp.bfloat16)
    cot_z = (d_features[3 * fields : 4 * fields] + d_advect * vel_z).astype(jnp.bfloat16)
    velocity = jnp.stack(
        [
            jnp.sum(d_advect * grad_xf, axis=0),
            jnp.sum(d_advect * grad_yf, axis=0),
            jnp.sum(d_advect * grad_zf, axis=0),
        ]
    )
    padded = jnp.concatenate([velocity, jnp.zeros((fields - 3, cells), jnp.float32)], axis=0)
    local = cot_f + d_features[0:fields] + padded
    return (updated, local, cot_x, cot_y, cot_z, w_in_part, b_in_part, w_out_part, b_out_part)


def line_product(operator, pencil):
    return jnp.einsum(
        "ia,tfajk->tfijk", operator, pencil, preferred_element_type=jnp.float32
    ).astype(jnp.bfloat16)


def streamwise_pass(field_set, operator):
    pencil = lax.all_to_all(field_set, "space", split_axis=3, concat_axis=2, tiled=True)
    derived = line_product(operator, pencil)
    return lax.all_to_all(derived, "space", split_axis=2, concat_axis=3, tiled=True)


def body(state, cotangent, x_operator, y_operator, z_operator, w_in, b_in, w_out, b_out):
    members, fields, x_planes, span, normal = state.shape
    cells = span * normal
    grad_y = jnp.einsum(
        "ja,tfiak->tfijk", y_operator, state, preferred_element_type=jnp.float32
    ).astype(jnp.bfloat16)
    grad_z = jnp.einsum(
        "ka,tfija->tfijk", z_operator, state, preferred_element_type=jnp.float32
    ).astype(jnp.bfloat16)
    grad_x = streamwise_pass(state, x_operator)
    anchor = jnp.int32(0)

    def take_row(source, member, plane):
        piece = lax.dynamic_slice(
            source, (member, anchor, plane, anchor, anchor), (1, fields, 1, span, normal)
        )
        return piece.reshape(fields, cells)

    def store_row(target, value, member, plane):
        shaped = value.reshape(1, fields, 1, span, normal)
        return lax.dynamic_update_slice(target, shaped, (member, anchor, plane, anchor, anchor))

    def plane_step(position, carried):
        updated_all, local_all, cotx_all, coty_all, cotz_all, totals = carried
        member = (position // x_planes).astype(jnp.int32)
        plane = (position % x_planes).astype(jnp.int32)
        result = row_work(
            take_row(state, member, plane),
            take_row(grad_x, member, plane),
            take_row(grad_y, member, plane),
            take_row(grad_z, member, plane),
            take_row(cotangent, member, plane),
            w_in,
            b_in,
            w_out,
            b_out,
        )
        updated_all = store_row(updated_all, result[0], member, plane)
        local_all = store_row(local_all, result[1], member, plane)
        cotx_all = store_row(cotx_all, result[2], member, plane)
        coty_all = store_row(coty_all, result[3], member, plane)
        cotz_all = store_row(cotz_all, result[4], member, plane)
        totals = (
            totals[0] + result[5],
            totals[1] + result[6],
            totals[2] + result[7],
            totals[3] + result[8],
        )
        return (updated_all, local_all, cotx_all, coty_all, cotz_all, totals)

    start_totals = (
        jnp.zeros(w_in.shape, jnp.float32),
        jnp.zeros(b_in.shape, jnp.float32),
        jnp.zeros(w_out.shape, jnp.float32),
        jnp.zeros(b_out.shape, jnp.float32),
    )
    start = (
        jnp.zeros(state.shape, jnp.bfloat16),
        jnp.zeros(state.shape, jnp.float32),
        jnp.zeros(state.shape, jnp.bfloat16),
        jnp.zeros(state.shape, jnp.bfloat16),
        jnp.zeros(state.shape, jnp.bfloat16),
        start_totals,
    )
    updated_all, local_all, cotx_all, coty_all, cotz_all, totals = lax.fori_loop(
        0, members * x_planes, plane_step, start
    )
    adjoint = local_all + streamwise_pass(cotx_all, x_operator.T).astype(jnp.float32)
    adjoint = adjoint + jnp.einsum(
        "aj,tfiak->tfijk", y_operator, coty_all, preferred_element_type=jnp.float32
    )
    adjoint = adjoint + jnp.einsum(
        "ak,tfija->tfijk", z_operator, cotz_all, preferred_element_type=jnp.float32
    )
    summed = lax.psum((totals[0], totals[1], totals[2], totals[3]), ("dp", "space"))
    total_cells = members * lax.axis_size("dp") * x_planes * lax.axis_size("space") * cells
    scaling = 1.0 / math.sqrt(total_cells)
    return (
        updated_all,
        adjoint.astype(jnp.bfloat16),
        summed[0] * scaling,
        summed[1] * scaling,
        summed[2] * scaling,
        summed[3] * scaling,
    )


def solution(mesh):
    return jax.shard_map(
        body,
        mesh=mesh,
        in_specs=(
            P("dp", None, "space", None, None),
            P("dp", None, "space", None, None),
            P(),
            P(),
            P(),
            P(),
            P(),
            P(),
            P(),
        ),
        out_specs=(
            P("dp", None, "space", None, None),
            P("dp", None, "space", None, None),
            P(),
            P(),
            P(),
            P(),
        ),
        check_vma=False,
    )
```

profile of v0, /device:TPU:1, one launch (start us, length us, event | category | flops | bytes accessed | tf_op | source)
XLA Modules:
  0.0 1003.9 jit_solution(8343891349614136507)
XLA Ops:
  0.6 4.4 copy.53
  5.0 97.8 %all_to_all.57 = bf16[1,5,16,96,192]{4,2,1,0,3:T(8,128)(2,1)S(1)} all-to-all(bf16[1,5,16,96,192]{4,2,1,0,3:T(8,128)(2,1)S(1)} %copy.53), channel_id=1, replica_groups=mesh['dp'=16,'space'=16] {'space'}, dimensions={3} | all-to-all | bytes 5898240 | tf_op jit(solution)/shard_map/all_to_all | solution.py:60
  105.1 8.8 copy.57
  113.8 4.7 all-to-all-start.1
  118.6 5.5 convert_bitcast_fusion.2
  124.1 3.1 convert_bitcast_fusion.1
  127.3 111.0 %all-to-all-done.1 = bf16[1,5,256,6,192]{4,3,1,0,2:T(8,128)(2,1)} async-done(((bf16[1,5,256,6,192]{4,3,1,0,2:T(8,128)(2,1)}), bf16[1,5,256,6,192]{4,3,1,0,2:T(8,128)(2,1)}, u32[]{:S(2)}, u32[]{:S(2)}) %all-to-all-start.1) | async-done | bytes 2949152 | tf_op jit(solution)/shard_map/all_to_all | solution.py:62
  238.3 3.4 copy.58
  242.3 3.4 copy.62
  245.6 2.4 broadcast.106.clone.2
  248.0 2.5 broadcast.106.clone.1
  250.5 2.4 broadcast.106.clone
  252.9 2.4 broadcast.106
  255.3 4.1 broadcast_in_dim.18.clone
  259.4 421.7 %while.32 = (s32[]{:T(128)}, bf16[1,5,16,96,192]{4,3,2,1,0:T(8,128)(2,1)}, f32[1,5,16,96,192]{3,4,2,1,0:T(8,128)}, bf16[1,5,16,96,192]{4,3,1,2,0:T(8,128)(2,1)},...) while((s32[]{:T(128)}, ...), condition=%wide.region_6.7_spmd.clone, body=%wide.region_0.6_spmd.clone.sunk | while | flops 197889232 | bytes 50562004 | solution.py:129
  265.1 1.6 convert_reduce_fusion.5
  274.8 2.0 reshape.199
  276.8 2.6 convolution_add_fusion.4
  301.1 2.0 reshape.199
  303.1 2.6 convolution_add_fusion.4
  327.5 2.0 reshape.199
  329.5 2.6 convolution_add_fusion.4
  353.8 2.0 reshape.199
  355.8 2.6 convolution_add_fusion.4
  370.5 1.6 convert_reduce_fusion.5
  380.2 2.0 reshape.199
  382.2 2.6 convolution_add_fusion.4
  406.5 2.0 reshape.199
  408.5 2.6 convolution_add_fusion.4
  423.2 1.6 convert_reduce_fusion.5
  432.9 2.0 reshape.199
  434.9 2.6 convolution_add_fusion.4
  449.5 1.6 convert_reduce_fusion.5
  459.2 2.0 reshape.199
  461.2 2.6 convolution_add_fusion.4
  475.8 1.6 convert_reduce_fusion.5
  485.5 2.0 reshape.199
  487.5 2.6 convolution_add_fusion.4
  502.1 1.6 convert_reduce_fusion.5
  511.8 2.0 reshape.199
  513.8 2.6 convolution_add_fusion.4
  538.2 2.0 reshape.199
  540.2 2.6 convolution_add_fusion.4
  564.5 2.0 reshape.199
  566.5 2.6 convolution_add_fusion.4
  590.8 2.0 reshape.199
  592.8 2.6 convolution_add_fusion.4
  617.2 2.0 reshape.199
  619.2 2.6 convolution_add_fusion.4
  643.5 2.0 reshape.199
  645.5 2.6 convolution_add_fusion.4
  669.9 2.0 reshape.199
  671.9 2.6 convolution_add_fusion.4
  681.1 4.3 copy.66
  685.5 91.7 %all_to_all.58 = bf16[1,5,16,96,192]{4,2,1,0,3:T(8,128)(2,1)S(1)} all-to-all(bf16[1,5,16,96,192]{4,2,1,0,3:T(8,128)(2,1)S(1)} %copy.66), channel_id=1, replica_groups=mesh['dp'=16,'space'=16] {'space'}, dimensions={3} | all-to-all | bytes 5898240 | tf_op jit(solution)/shard_map/all_to_all | solution.py:60
  779.3 8.8 copy.70
  788.1 4.7 all-to-all-start.3
  792.9 163.9 %all-reduce = (f32[64,20]{0,1:T(8,128)S(1)}, f32[64]{0:T(128)S(1)}, f32[5,64]{1,0:T(8,128)S(1)}, f32[5]{0:T(128)S(1)}) all-reduce(f32[64,20]{0,1:T(8,128)S(1)} %copy-done.20, f32[64]{0:T(128)S(1)} %get-tuple-element.893, f32[5,64]{1,0:T(8,128)S(1)} %get-tuple-element.894, ...), channel_id=1, replica_groups=mesh['dp'=16,'space'=16] {'dp','space'}, use_global_device_ids=true, to_apply=%region_7.8 | all-reduce | flops 1669 | bytes 13352 | tf_op jit(solution)/shard_map/psum | solution.py:139
  959.0 6.6 fusion.25
  965.6 3.4 copy.71
  970.1 4.5 copy.72
  974.6 9.9 copy.74
  984.5 12.9 %fusion.24 = bf16[1,5,16,96,192]{3,4,2,1,0:T(8,128)(2,1)} fusion(f32[5,16,192,96]{3,2,1,0:T(8,128)} %fusion.25, f32[1,5,16,96,192]{3,4,2,1,0:T(8,128)} %get-tuple-element.888, f32[1,5,16,96,192]{3,4,2,1,0:T(8,128)} %copy.74, bf16[192,192]{1,0:T(8,128)(2,1)S(1)} %copy-done.12, bf16[1,5,16,96,192]{4,3,1,2,0:T(8,128)(2,1)} %get-tuple-element.891), kind=kOutput, calls=%fused_computation.55 | convolution fusion | flops 572129280 | bytes 23666688 | tf_op jit(solution)/shard_map/ak,tfija->tfijk/dot_general | solution.py:136
  997.4 6.4 copy.79
  (945 shorter events, 342.5 us)
Async XLA Ops:
  0.6 103.1 %copy-start = (bf16[256,256]{1,0:T(8,128)(2,1)S(1)}, bf16[256,256]{1,0:T(8,128)(2,1)}, u32[]{:S(2)}) copy-start(bf16[256,256]{1,0:T(8,128)(2,1)} %param.13) | copy-start | bytes 393220
  113.8 4.8 copy-start.14
  113.8 124.5 %all-to-all-start.1 = ((bf16[1,5,256,6,192]{4,3,1,0,2:T(8,128)(2,1)}), bf16[1,5,256,6,192]{4,3,1,0,2:T(8,128)(2,1)}, u32[]{:S(2)}, u32[]{:S(2)}) async-start(bf16[1,5,256,6,192]{4,3,1,0,2:T(8,128)(2,1)} %copy.57), calls=%async_computation.1 | async-start | bytes 10485760 | tf_op jit(solution)/shard_map/all_to_all | solution.py:62
  118.6 5.6 copy-start.4
  118.6 5.5 copy-start.11
  255.3 4.1 copy-start.10
  255.3 4.1 copy-start.13
  255.3 4.1 copy-start.16
  255.3 4.1 copy-start.17
  264.8 7.5 copy-start.1
  265.1 7.2 copy-start.2
  281.0 5.0 copy-start.18
  291.1 7.6 copy-start.1
  291.4 7.2 copy-start.2
  307.3 5.0 copy-start.18
  317.5 7.6 copy-start.1
  317.8 7.2 copy-start.2
  333.7 5.0 copy-start.18
  343.8 7.6 copy-start.1
  344.1 7.2 copy-start.2
  360.0 5.1 copy-start.18
  370.2 7.6 copy-start.1
  370.5 7.2 copy-start.2
  385.8 4.1 copy-start.5
  386.4 5.1 copy-start.18
  396.5 7.6 copy-start.1
  396.8 7.2 copy-start.2
  412.7 5.0 copy-start.18
  422.8 7.6 copy-start.1
  423.2 7.2 copy-start.2
  439.0 5.0 copy-start.18
  449.2 7.6 copy-start.1
  449.5 7.2 copy-start.2
  465.4 5.0 copy-start.18
  475.5 7.6 copy-start.1
  475.8 7.2 copy-start.2
  491.7 5.0 copy-start.18
  501.8 7.6 copy-start.1
  502.1 7.2 copy-start.2
  518.0 5.0 copy-start.18
  528.2 7.6 copy-start.1
  528.5 7.2 copy-start.2
  544.4 5.0 copy-start.18
  554.5 7.6 copy-start.1
  554.8 7.2 copy-start.2
  570.7 5.0 copy-start.18
  580.8 7.6 copy-start.1
  581.1 7.2 copy-start.2
  596.5 4.1 copy-start.5
  597.0 5.1 copy-start.18
  607.2 7.6 copy-start.1
  607.5 7.2 copy-start.2
  623.4 5.0 copy-start.18
  633.5 7.6 copy-start.1
  633.8 7.2 copy-start.2
  649.2 4.1 copy-start.5
  649.7 5.1 copy-start.18
  659.9 7.6 copy-start.1
  660.2 7.2 copy-start.2
  676.1 5.0 copy-start.18
  788.1 4.7 copy-start.20
  788.1 170.9 %copy-start.15 = (bf16[96,96]{1,0:T(8,128)(2,1)S(1)}, bf16[96,96]{1,0:T(8,128)(2,1)}, u32[]{:S(2)}) copy-start(bf16[96,96]{1,0:T(8,128)(2,1)} %param.14) | copy-start | bytes 55300
  788.1 177.4 %all-to-all-start.3 = ((bf16[1,5,256,6,192]{4,3,1,0,2:T(8,128)(2,1)}), bf16[1,5,256,6,192]{4,3,1,0,2:T(8,128)(2,1)}, u32[]{:S(2)}, u32[]{:S(2)}) async-start(bf16[1,5,256,6,192]{4,3,1,0,2:T(8,128)(2,1)} %copy.70), calls=%async_computation.3 | async-start | bytes 10485760 | tf_op jit(solution)/shard_map/all_to_all | solution.py:62
  974.6 9.9 copy-start.12
  (109 other events, 159.0 us)
where the time goes:
time: 1010 us; the launch traced here: 1000 us
  blocking collectives  353 us (35%)
  local copies, waits for them, and re-layouts  314 us (31%)
  matrix products  145 us (14%)
  waiting for transfers between devices  111 us (11%)
  other arithmetic  66.4 us (7%)
    all_to_all x2, blocking collectives, streamwise_pass(): lax.all_to_all(field_set, 'space', split_axis=3, concat_axis=2, tiled=True)  189 us
    psum x1, blocking collectives, body(): lax.psum((totals[0], totals[1], totals[2], totals[3]), ('dp', 'space'))  164 us
    all_to_all x2, waiting for transfers between devices, streamwise_pass(): lax.all_to_all(derived, 'space', split_axis=2, concat_axis=3, tiled=True)  111 us
    dynamic_update_slice x96, local copies, waits for them, and re-layouts, store_row(): lax.dynamic_update_slice(target, shaped, (member, anchor, plane, anchor,...  62.5 us
    reshape x80, local copies, waits for them, and re-layouts, store_row(): shaped = value.reshape(1, fields, 1, span, normal)  49.3 us
    dynamic_slice x64, local copies, waits for them, and re-layouts, take_row(): lax.dynamic_slice(source, (member, anchor, plane, anchor, anchor), (1, fi...  48.9 us
    dot_general x16, matrix products, row_work(): jnp.dot(d_before, features.T, preferred_element_type=jnp.float32)  42.3 us
    another operation x48, local copies, waits for them, and re-layouts, row_work(): jnp.stack([jnp.sum(d_advect * grad_xf, axis=0), jnp.sum(d_advect * grad_y...  36.1 us
  transfers between devices with their start and end apart: 2, of which 1 were waited for; matrix products, arithmetic and copies ran while one was open for 2% of the time, Pallas kernels for 0%

commit v1 on v0

v1 whole, which is shorter than its diff:
```python
import functools
import math

import jax
import jax.numpy as jnp
from jax import lax
from jax.experimental import pallas as pl
from jax.experimental.pallas import tpu as pltpu
from jax.sharding import PartitionSpec as P

MESH = pl.DeviceIdType.MESH
F32 = jnp.float32
BF16 = jnp.bfloat16
GROUP = 16
FIELDS = 5
HIDDEN = 64
PACK = 384
WIDE = 768
CHUNKS = 3
CHANNELS = 4 * FIELDS
EXTENDED = CHANNELS + 3


def pack(a, b):
    tail = jnp.concatenate([a[..., 128:192], b[..., 128:192]], axis=-1)
    return jnp.concatenate([a[..., 0:128], b[..., 0:128], tail], axis=-1)


def unpack(p):
    a = jnp.concatenate([p[..., 0:128], p[..., 256:320]], axis=-1)
    b = jnp.concatenate([p[..., 128:256], p[..., 320:384]], axis=-1)
    return a, b


def widen(v):
    return jnp.concatenate([v[:, 0:8], v[:, 8:16]], axis=-1)


def narrow(v):
    return jnp.concatenate([v[..., 0:PACK], v[..., PACK:WIDE]], axis=1)


def dot(a, b):
    return jnp.dot(a, b, preferred_element_type=F32)


def dot_t(a, b):
    return lax.dot_general(a, b, (((1,), (1,)), ((), ())), preferred_element_type=F32)


def step_kernel(
    s_ref, c_ref, x_ref, xt_ref, y_ref, yt_ref, z_ref, zt_ref, perm_ref,
    w1_ref, w1t_ref, w2_ref, w2t_ref, bo_ref,
    ns_ref, sg_ref, g1_ref, g2_ref, g3_ref,
    send, pen, recv, gx, gy, gz, cx, cy, cz, loc, ssem, rsem, lsem,
):
    me = lax.axis_index("space")

    def copy_of(phase, c, s, target):
        dst = lax.rem(me + s, GROUP)
        return pltpu.make_async_remote_copy(
            src_ref=send.at[c, dst],
            dst_ref=target.at[c, me],
            send_sem=ssem.at[phase, c, s],
            recv_sem=rsem.at[phase, c, s],
            device_id={"space": dst},
            device_id_type=MESH,
        )

    def own_of(phase, c, target):
        return pltpu.make_async_copy(send.at[c, me], target.at[c, me], lsem.at[phase, c])

    def start(phase, c, target):
        own_of(phase, c, target).start()

        def one(s, carry):
            copy_of(phase, c, s, target).start()
            return carry

        lax.fori_loop(1, GROUP, one, 0)

    def finish(phase, c, target):
        own_of(phase, c, target).wait()

        def one(s, carry):
            copy_of(phase, c, s, target).wait()
            return carry

        lax.fori_loop(1, GROUP, one, 0)

    def rows(c, half):
        return pl.ds(pl.multiple_of(c * 32 + 16 * half, 16), 16)

    barrier = pltpu.get_barrier_semaphore()

    def greet(s, carry):
        pl.semaphore_signal(
            barrier, inc=1, device_id={"space": lax.rem(me + s, GROUP)}, device_id_type=MESH
        )
        return carry

    lax.fori_loop(1, GROUP, greet, 0)
    pl.semaphore_wait(barrier, GROUP - 1)

    def send_state(c, carry):
        for f in range(FIELDS):
            a = s_ref[f, :, rows(c, 0), :].reshape(256, 192)
            b = s_ref[f, :, rows(c, 1), :].reshape(256, 192)
            moved = dot(perm_ref[...], pack(a, b)).astype(BF16)
            send[c, :, :, f * PACK : (f + 1) * PACK] = moved.reshape(16, 16, PACK)
        start(0, c, pen)
        return carry

    lax.fori_loop(0, CHUNKS, send_state, 0)

    def lines(a, carry):
        for f in range(FIELDS):
            s = s_ref[f, a]
            dy = dot(y_ref[...], s).astype(BF16)
            dz = dot(s, zt_ref[...]).astype(BF16)
            for c in range(CHUNKS):
                lo, mid, hi = 32 * c, 32 * c + 16, 32 * c + 32
                gy[c, f, a] = pack(dy[lo:mid], dy[mid:hi])
                gz[c, f, a] = pack(dz[lo:mid], dz[mid:hi])
        return carry

    lax.fori_loop(0, GROUP, lines, 0)

    g1_ref[...] = jnp.zeros_like(g1_ref)
    g2_ref[...] = jnp.zeros_like(g2_ref)
    g3_ref[...] = jnp.zeros_like(g3_ref)

    def streamwise(c, operator):
        for f in range(FIELDS):
            lanes = slice(f * PACK, (f + 1) * PACK)
            done = dot(operator[...], pen[c, :, :, lanes].reshape(256, PACK)).astype(BF16)
            send[c, :, :, lanes] = done.reshape(16, 16, PACK)

    def forward_lines(c, carry):
        finish(0, c, pen)
        streamwise(c, x_ref)
        start(1, c, recv)
        return carry

    lax.fori_loop(0, CHUNKS, forward_lines, 0)

    def closure(c, a):
        state = pack(s_ref[:, a, rows(c, 0), :], s_ref[:, a, rows(c, 1), :])
        cot = pack(c_ref[:, a, rows(c, 0), :], c_ref[:, a, rows(c, 1), :])
        features = widen(
            jnp.concatenate([state, gx[:, a], gy[c, :, a], gz[c, :, a]], axis=0).astype(F32)
        )
        cw = widen(cot.astype(F32))
        ones = jnp.ones((3, 8, WIDE), F32)
        fb = jnp.concatenate([features, ones], axis=0).reshape(EXTENDED * 8, WIDE).astype(BF16)
        active = jnp.tanh(dot(w1_ref[...], fb))
        hidden = active.astype(BF16)
        closed = dot(w2_ref[...], hidden).reshape(FIELDS, 8, WIDE)
        half = 0.5 * cw
        d_closure = half.reshape(FIELDS * 8, WIDE).astype(BF16)
        d_hidden = dot(w2t_ref[...], d_closure)
        d_before = (d_hidden * (1.0 - active * active)).astype(BF16)
        d_features = dot(w1t_ref[...], d_before).reshape(CHANNELS, 8, WIDE)
        g1_ref[...] += dot_t(d_before, fb)
        g2_ref[...] += dot_t(hidden, d_closure)
        dc = d_closure.astype(F32)
        g3_ref[...] += sum(dc[:, 128 * t : 128 * (t + 1)] for t in range(WIDE // 128))
        u, v, w = features[0:1], features[1:2], features[2:3]
        fx, fy, fz = features[5:10], features[10:15], features[15:20]
        advect = u * fx + v * fy + w * fz
        bias = jnp.stack([jnp.full((8, WIDE), bo_ref[f], F32) for f in range(FIELDS)])
        updated = narrow(features[0:5] + 0.5 * (closed + bias - advect)).astype(BF16)
        first, second = unpack(updated)
        ns_ref[:, a, rows(c, 0), :] = first
        ns_ref[:, a, rows(c, 1), :] = second
        cx[:, a] = narrow(d_features[5:10] - half * u).astype(BF16)
        cy[c, :, a] = narrow(d_features[10:15] - half * v).astype(BF16)
        cz[c, :, a] = narrow(d_features[15:20] - half * w).astype(BF16)
        vel = [-jnp.sum(half * g, axis=0, keepdims=True) for g in (fx, fy, fz)]
        padded = jnp.concatenate(vel + [jnp.zeros((2, 8, WIDE), F32)], axis=0)
        loc[c, :, a] = narrow(cw + d_features[0:5] + padded)

    def backward_lines(c):
        finish(2, c, pen)
        streamwise(c, xt_ref)
        start(3, c, recv)

    def middle(c, carry):
        finish(1, c, recv)
        for f in range(FIELDS):
            lanes = slice(f * PACK, (f + 1) * PACK)
            back = dot(perm_ref[...], recv[c, :, :, lanes].reshape(256, PACK)).astype(BF16)
            gx[f] = back.reshape(16, 16, PACK)

        def plane(a, inner):
            closure(c, a)
            return inner

        lax.fori_loop(0, GROUP, plane, 0)
        for f in range(FIELDS):
            lanes = slice(f * PACK, (f + 1) * PACK)
            moved = dot(perm_ref[...], cx[f].reshape(256, PACK)).astype(BF16)
            send[c, :, :, lanes] = moved.reshape(16, 16, PACK)
        start(2, c, pen)

        @pl.when(c >= 1)
        def _():
            backward_lines(c - 1)

        return carry

    lax.fori_loop(0, CHUNKS, middle, 0)

    def adjoint_lines(a, carry):
        for f in range(FIELDS):
            ys, zs = [], []
            for c in range(CHUNKS):
                ys += unpack(cy[c, f, a])
                zs += unpack(cz[c, f, a])
            total = dot(yt_ref[...], jnp.concatenate(ys, axis=0))
            total += dot(jnp.concatenate(zs, axis=0), z_ref[...])
            for c in range(CHUNKS):
                lo, mid, hi = 32 * c, 32 * c + 16, 32 * c + 32
                loc[c, f, a] += pack(total[lo:mid], total[mid:hi])
        return carry

    lax.fori_loop(0, GROUP, adjoint_lines, 0)
    backward_lines(CHUNKS - 1)

    def last(c, carry):
        finish(3, c, recv)
        for f in range(FIELDS):
            lanes = slice(f * PACK, (f + 1) * PACK)
            back = dot(perm_ref[...], recv[c, :, :, lanes].reshape(256, PACK))
            whole = (back.reshape(16, 16, PACK) + loc[c, f]).astype(BF16)
            first, second = unpack(whole)
            sg_ref[f, :, rows(c, 0), :] = first
            sg_ref[f, :, rows(c, 1), :] = second
        return carry

    lax.fori_loop(0, CHUNKS, last, 0)


def spread(w):
    n, m = w.shape
    eye = jnp.eye(8, dtype=w.dtype)
    return (w[:, None, :, None] * eye[None, :, None, :]).reshape(n * 8, m * 8)


def gather(g, n, m):
    eye = jnp.eye(8, dtype=F32)
    return jnp.sum(g.reshape(n, 8, m, 8) * eye[None, :, None, :], axis=(1, 3))


def body(state, cotangent, x_operator, y_operator, z_operator, w_in, b_in, w_out, b_out):
    shape = state.shape[1:]
    hi = lax.reduce_precision(b_in, 8, 7)
    mid = lax.reduce_precision(b_in - hi, 8, 7)
    low = b_in - hi - mid
    columns = jnp.stack([hi, mid, low], axis=1).astype(BF16)
    w1 = spread(jnp.concatenate([w_in, columns], axis=1))
    w1t = spread(w_in.T)
    w2 = spread(w_out)
    w2t = spread(w_out.T)
    place = jnp.arange(256)
    swapped = (place % 16) * 16 + place // 16
    perm = (swapped[:, None] == place[None, :]).astype(BF16)
    vmem = pl.BlockSpec(memory_space=pltpu.VMEM)
    buffer = pltpu.VMEM((CHUNKS, GROUP, GROUP, FIELDS * PACK), BF16)
    packed = pltpu.VMEM((CHUNKS, FIELDS, GROUP, GROUP, PACK), BF16)
    part = pltpu.VMEM((FIELDS, GROUP, GROUP, PACK), BF16)
    ns, sg, g1, g2, g3 = pl.pallas_call(
        step_kernel,
        out_shape=(
            jax.ShapeDtypeStruct(shape, BF16),
            jax.ShapeDtypeStruct(shape, BF16),
            jax.ShapeDtypeStruct((HIDDEN * 8, EXTENDED * 8), F32),
            jax.ShapeDtypeStruct((HIDDEN * 8, FIELDS * 8), F32),
            jax.ShapeDtypeStruct((FIELDS * 8, 128), F32),
        ),
        in_specs=[vmem] * 13 + [pl.BlockSpec(memory_space=pltpu.SMEM)],
        out_specs=[vmem] * 5,
        scratch_shapes=[
            buffer, buffer, buffer, part, packed, packed, part, packed, packed,
            pltpu.VMEM((CHUNKS, FIELDS, GROUP, GROUP, PACK), F32),
            pltpu.SemaphoreType.DMA((4, CHUNKS, GROUP)),
            pltpu.SemaphoreType.DMA((4, CHUNKS, GROUP)),
            pltpu.SemaphoreType.DMA((4, CHUNKS)),
        ],
        compiler_params=pltpu.CompilerParams(
            collective_id=0, has_side_effects=True, vmem_limit_bytes=60 * 1024 * 1024
        ),
        cost_estimate=pl.CostEstimate(flops=10**11, bytes_accessed=2 * 10**7, transcendentals=2 * 10**7),
        name="evolution",
    )(
        state[0], cotangent[0], x_operator, x_operator.T, y_operator, y_operator.T,
        z_operator, z_operator.T, perm, w1, w1t, w2, w2t, b_out,
    )
    w_in_all = gather(g1, HIDDEN, EXTENDED)
    w_out_all = gather(g2, HIDDEN, FIELDS).T
    b_out_all = jnp.sum(g3.reshape(FIELDS, 8 * 128), axis=1)
    summed = lax.psum((w_in_all, w_out_all, b_out_all), ("dp", "space"))
    cells = (
        lax.axis_size("dp") * lax.axis_size("space") * shape[1] * shape[2] * shape[3]
    )
    scaling = 1.0 / math.sqrt(cells)
    return (
        ns[None],
        sg[None],
        summed[0][:, 0:CHANNELS] * scaling,
        summed[0][:, CHANNELS] * scaling,
        summed[1] * scaling,
        summed[2] * scaling,
    )


def solution(mesh):
    wide = P("dp", None, "space", None, None)
    return jax.shard_map(
        body,
        mesh=mesh,
        in_specs=(wide, wide) + (P(),) * 7,
        out_specs=(wide, wide) + (P(),) * 4,
        check_vma=False,
    )
```

time: 1010 us -> 403 us (0.40)
  local copies, waits for them, and re-layouts: 314 us -> 34.8 us
  Pallas kernels: 0 us -> 275 us
  blocking collectives: 353 us -> 80.6 us
  matrix products: 145 us -> 0 us
  waiting for transfers between devices: 111 us -> 0 us
  other arithmetic: 66.4 us -> 11 us
    pallas_call x0 -> x1, Pallas kernels: none -> 275 us  [body(): pl.pallas_call(step_kernel, out_shape=(jax.ShapeDtypeStruct(shape, BF16),...]
    all_to_all x2 -> x0, blocking collectives: 189 us -> none  [streamwise_pass(): lax.all_to_all(field_set, 'space', split_axis=3, concat_axis=2, tiled=True)]
    dot_general x102 -> x0, matrix products: 145 us -> none  [the longest x16 42.3 us: row_work(): jnp.dot(d_before, features.T, preferred_element_type=jnp.float32)]
    all_to_all x2 -> x0, waiting for transfers between devices: 111 us -> none  [streamwise_pass(): lax.all_to_all(derived, 'space', split_axis=2, concat_axis=3, tiled=True)]
    psum x1, blocking collectives: 164 us -> 80.6 us  [body(): summed = lax.psum((w_in_all, w_out_all, b_out_all), ('dp', 'space'))]
    dynamic_update_slice x96 -> x0, local copies, waits for them, and re-layouts: 62.5 us -> none  [store_row(): lax.dynamic_update_slice(target, shaped, (member, anchor, plane, anchor,...]
    reshape x144 -> x2, local copies, waits for them, and re-layouts: 68.6 us -> 6.81 us  [gather(): return jnp.sum(g.reshape(n, 8, m, 8) * eye[None, :, None, :], axis=(1, 3))]
    dynamic_slice x64 -> x0, local copies, waits for them, and re-layouts: 48.9 us -> none  [take_row(): lax.dynamic_slice(source, (member, anchor, plane, anchor, anchor), (1, fi...]
  transfers between devices with their start and end apart: 2 -> 0, of which waited for: 1 -> 0; matrix products, arithmetic and copies ran while one was open for 2% -> 0% of each run, Pallas kernels for 0% -> 0%
where the time goes in v1:
time: 403 us; the launch traced here: 402 us
  Pallas kernels  275 us (68%)
  blocking collectives  80.6 us (20%)
  local copies, waits for them, and re-layouts  34.8 us (9%)
  other arithmetic  11 us (3%)
    pallas_call x1, Pallas kernels, body(): pl.pallas_call(step_kernel, out_shape=(jax.ShapeDtypeStruct(shape, BF16),...  275 us
    psum x1, blocking collectives, body(): summed = lax.psum((w_in_all, w_out_all, b_out_all), ('dp', 'space'))  80.6 us
    mul x6, local copies, waits for them, and re-layouts, spread(): return (w[:, None, :, None] * eye[None, :, None, :]).reshape(n * 8, m * 8)  14.3 us
    unnamed x9, local copies, waits for them, and re-layouts  11.2 us

profile of v1, /device:TPU:1, one launch (start us, length us, event | category | flops | bytes accessed | tf_op | source)
XLA Modules:
  0.0 402.3 jit_solution(13211438077806947104)
XLA Ops:
  0.6 0.0 copy-start.1
  0.7 0.7 fusion.7
  1.3 0.1 copy.23
  1.4 0.7 pad_maximum_fusion
  2.1 1.4 copy.21
  3.6 1.6 copy.22
  5.2 0.8 fusion.perm_ref
  5.9 1.7 copy.20
  7.6 0.8 broadcast_multiply_fusion.3
  8.4 1.5 mul.128.w2_ref
  9.9 0.8 broadcast_multiply_fusion.2
  10.7 0.9 mul.132
  11.6 0.8 copy.26.w2t_ref
  12.3 0.0 copy-done.1
  12.3 0.2 broadcast_multiply_fusion.1
  12.6 4.7 %mul.124.w1t_ref = bf16[160,512]{1,0:T(8,128)(2,1)} reshape(bf16[20,8,64,8]{3,2,1,0:T(8,128)(2,1)S(1)} %broadcast_multiply_fusion.1) | data formatting | bytes 327680 | tf_op jit(solution)/shard_map/mul | solution.py:247
  17.3 0.3 broadcast_multiply_fusion
  17.6 5.7 %mul.120 = bf16[512,184]{0,1:T(8,128)(2,1)S(1)} reshape(bf16[64,8,23,8]{1,0,3,2:T(8,128)(2,1)S(1)} %broadcast_multiply_fusion) | data formatting | bytes 376832 | tf_op jit(solution)/shard_map/mul | solution.py:247
  23.2 0.8 copy.25.w1_ref
  24.1 275.1 %evolution.1 = (bf16[5,16,96,192]{3,2,1,0:T(8,128)(2,1)}, bf16[5,16,96,192]{3,2,1,0:T(8,128)(2,1)}, f32[512,184]{1,0:T(8,128)}, f32[512,40]{1,0:T(8,128)}, f32[40,128]{1,0:T(8,128)}) custom-call(bf16[5,16,96,192]{3,2,1,0:T(8,128)(2,1)} %bitcast.42, bf16[5,16,96,192]{3,2,1,0:T(8,128)(2,1)} %bitcast.43, bf16[256,256]{1,0:T(8,128)(2,1)} %x_ref.1, ...), custom_call_target="tpu_custom_call" | custom-call | flops 99999997952 | bytes 20000000 | tf_op jit(solution)/shard_map/evolution/pallas_call | solution.py:272
  299.2 0.8 reduce_sum.36
  300.0 0.1 reduce_sum.37
  300.1 0.1 reduce_sum.38
  300.2 1.1 copy.28
  301.3 1.2 copy.27
  302.5 0.7 reshape.78
  303.3 0.2 multiply_reduce_fusion.1
  303.5 6.1 %reshape.77 = f32[64,8,23,8]{1,0,3,2:T(8,128)} reshape(f32[512,184]{0,1:T(8,128)S(1)} %copy.27) | data formatting | bytes 753664 | tf_op jit(solution)/shard_map/reshape | solution.py:252
  309.6 3.4 multiply_reduce_fusion
  312.9 80.6 %all-reduce = (f32[64,23]{0,1:T(8,128)S(1)}, f32[5,64]{1,0:T(8,128)S(1)}, f32[5]{0:T(128)S(1)}) all-reduce(f32[64,23]{0,1:T(8,128)S(1)} %multiply_reduce_fusion, f32[5,64]{1,0:T(8,128)S(1)} %bitcast.40, f32[5]{0:T(128)S(1)} %reduce_sum.38), channel_id=1, replica_groups=mesh['dp'=16,'space'=16] {'dp','space'}, use_global_device_ids=true, to_apply=%region_1.2 | all-reduce | flops 1797 | bytes 14376 | tf_op jit(solution)/shard_map/psum | solution.py:302
  393.5 0.6 broadcast_multiply_fusion.4
  394.1 0.5 broadcast_multiply_fusion.5
  394.6 0.5 fusion.11
  395.1 0.6 slice_multiply_fusion
  395.7 0.0 copy-start
  395.7 4.6 %copy.31 = bf16[1,5,16,96,192]{4,3,2,1,0:T(8,128)(2,1)} copy(bf16[1,5,16,96,192]{4,3,2,1,0:T(8,128)(2,1)} %bitcast.35) | data formatting | bytes 5898240
  400.3 0.0 copy-done
  400.3 1.9 copy.32
  (3 shorter events, 0.0 us)
Async XLA Ops:
  0.6 11.7 %copy-start.1 = (bf16[64,20]{0,1:T(8,128)(2,1)S(1)}, bf16[64,20]{0,1:T(8,128)(2,1)}, u32[]{:S(2)}) copy-start(bf16[64,20]{0,1:T(8,128)(2,1)} %param.14) | copy-start | bytes 7684
  395.7 4.6 %copy-start = (bf16[5,16,96,192]{3,2,1,0:T(8,128)(2,1)S(1)}, bf16[5,16,96,192]{3,2,1,0:T(8,128)(2,1)}, u32[]{:S(2)}) copy-start(bf16[5,16,96,192]{3,2,1,0:T(8,128)(2,1)} %get-tuple-element.12) | copy-start | bytes 8847364

commit v2 on v1

--- a/solution.py
+++ b/solution.py
@@ -48,13 +48,31 @@
     return lax.dot_general(a, b, (((1,), (1,)), ((), ())), preferred_element_type=F32)
 
 
+def iota(shape, axis):
+    return lax.broadcasted_iota(jnp.int32, shape, axis)
+
+
+def where_equal(shape, left, right):
+    return jnp.where(left(iota(shape, 0)) == right(iota(shape, 1)), 1.0, 0.0)
+
+
+def same(i):
+    return i
+
+
+def eighth(i):
+    return i // 8
+
+
 def step_kernel(
-    s_ref, c_ref, x_ref, xt_ref, y_ref, yt_ref, z_ref, zt_ref, perm_ref,
-    w1_ref, w1t_ref, w2_ref, w2t_ref, bo_ref,
-    ns_ref, sg_ref, g1_ref, g2_ref, g3_ref,
-    send, pen, recv, gx, gy, gz, cx, cy, cz, loc, ssem, rsem, lsem,
+    s_hbm, c_hbm, x_ref, y_ref, z_ref, wi_ref, wit_ref, b_ref, wo_ref, wot_ref, bo_ref,
+    ns_hbm, sg_hbm, total_ref,
+    s_ref, c_ref, ns_ref, xt_ref, yt_ref, zt_ref, perm_ref, w1_ref, w1t_ref, w2_ref, w2t_ref,
+    g1_ref, g2_ref, g3_ref, pay, slots, piece, ssem, rsem, lsem, msem, nsem, iosem,
+    send, pen, recv, gx, gy, gz, cx, cy, cz, loc,
 ):
     me = lax.axis_index("space")
+    team = lax.axis_index("dp")
 
     def copy_of(phase, c, s, target):
         dst = lax.rem(me + s, GROUP)
@@ -70,39 +88,68 @@
     def own_of(phase, c, target):
         return pltpu.make_async_copy(send.at[c, me], target.at[c, me], lsem.at[phase, c])
 
+    def each(one):
+        def run(s, carry):
+            one(s)
+            return carry
+
+        lax.fori_loop(1, GROUP, run, 0)
+
     def start(phase, c, target):
         own_of(phase, c, target).start()
-
-        def one(s, carry):
-            copy_of(phase, c, s, target).start()
-            return carry
-
-        lax.fori_loop(1, GROUP, one, 0)
+        each(lambda s: copy_of(phase, c, s, target).start())
 
     def finish(phase, c, target):
         own_of(phase, c, target).wait()
-
-        def one(s, carry):
-            copy_of(phase, c, s, target).wait()
-            return carry
-
-        lax.fori_loop(1, GROUP, one, 0)
+        each(lambda s: copy_of(phase, c, s, target).wait())
 
     def rows(c, half):
         return pl.ds(pl.multiple_of(c * 32 + 16 * half, 16), 16)
 
+    def chunk(c):
+        return pl.ds(pl.multiple_of(c * 32, 32), 32)
+
+    def load_state(c):
+        return pltpu.make_async_copy(
+            s_hbm.at[:, :, chunk(c), :], s_ref.at[:, :, chunk(c), :], iosem.at[0, c]
+        )
+
+    def load_cotangent(c):
+        return pltpu.make_async_copy(
+            c_hbm.at[:, :, chunk(c), :], c_ref.at[:, :, chunk(c), :], iosem.at[1, c]
+        )
+
+    def store_state(c):
+        return pltpu.make_async_copy(
+            ns_ref.at[:, :, chunk(c), :], ns_hbm.at[:, :, chunk(c), :], iosem.at[2, c]
+        )
+
+    def store_grad(c):
+        return pltpu.make_async_copy(
+            s_ref.at[:, :, chunk(c), :], sg_hbm.at[:, :, chunk(c), :], iosem.at[3, c]
+        )
+
+    for c in range(CHUNKS):
+        load_state(c).start()
+    for c in range(CHUNKS):
+        load_cotangent(c).start()
+
     barrier = pltpu.get_barrier_semaphore()
-
-    def greet(s, carry):
-        pl.semaphore_signal(
-            barrier, inc=1, device_id={"space": lax.rem(me + s, GROUP)}, device_id_type=MESH
-        )
-        return carry
-
-    lax.fori_loop(1, GROUP, greet, 0)
-    pl.semaphore_wait(barrier, GROUP - 1)
+    for axis, mine in (("space", me), ("dp", team)):
+
+        def greet(s, axis=axis, mine=mine):
+            pl.semaphore_signal(
+                barrier, inc=1, device_id={axis: lax.rem(mine + s, GROUP)}, device_id_type=MESH
+            )
+
+        each(greet)
+    perm_ref[...] = where_equal(
+        (256, 256), lambda i: (i % 16) * 16 + i // 16, same
+    ).astype(BF16)
+    pl.semaphore_wait(barrier, 2 * (GROUP - 1))
 
     def send_state(c, carry):
+        load_state(c).wait()
         for f in range(FIELDS):
             a = s_ref[f, :, rows(c, 0), :].reshape(256, 192)
             b = s_ref[f, :, rows(c, 1), :].reshape(256, 192)
@@ -112,6 +159,35 @@
         return carry
 
     lax.fori_loop(0, CHUNKS, send_state, 0)
+
+    for source, target in ((x_ref, xt_ref), (y_ref, yt_ref), (z_ref, zt_ref)):
+        unit = where_equal(source.shape, same, same).astype(BF16)
+        target[...] = dot_t(unit, source[...]).astype(BF16)
+
+    def spread(w):
+        n, m = w.shape
+        left = where_equal((n * 8, n), eighth, same).astype(BF16)
+        right = where_equal((m, m * 8), same, eighth).astype(BF16)
+        return dot(left, dot(w, right).astype(BF16)) * diagonal((n * 8, m * 8))
+
+    def diagonal(shape):
+        return where_equal(shape, lambda i: i % 8, lambda i: i % 8)
+
+    bias = b_ref[...]
+    high = bias.astype(BF16).astype(F32)
+    mid = (bias - high).astype(BF16).astype(F32)
+    low = bias - high - mid
+    places = iota((HIDDEN, EXTENDED * 8), 1) // 8
+    right = where_equal((CHANNELS, EXTENDED * 8), same, eighth).astype(BF16)
+    inner = dot(wi_ref[...], right)
+    for place, column in enumerate((high, mid, low)):
+        inner += jnp.where(places == CHANNELS + place, column, 0.0)
+    left = where_equal((HIDDEN * 8, HIDDEN), eighth, same).astype(BF16)
+    w1 = dot(left, inner.astype(BF16)) * diagonal((HIDDEN * 8, EXTENDED * 8))
+    w1_ref[...] = w1.astype(BF16)
+    w1t_ref[...] = spread(wit_ref[...]).astype(BF16)
+    w2_ref[...] = spread(wo_ref[...]).astype(BF16)
+    w2t_ref[...] = spread(wot_ref[...]).astype(BF16)
 
     def lines(a, carry):
         for f in range(FIELDS):
@@ -187,6 +263,7 @@
 
     def middle(c, carry):
         finish(1, c, recv)
+        load_cotangent(c).wait()
         for f in range(FIELDS):
             lanes = slice(f * PACK, (f + 1) * PACK)
             back = dot(perm_ref[...], recv[c, :, :, lanes].reshape(256, PACK)).astype(BF16)
@@ -202,6 +279,7 @@
             moved = dot(perm_ref[...], cx[f].reshape(256, PACK)).astype(BF16)
             send[c, :, :, lanes] = moved.reshape(16, 16, PACK)
         start(2, c, pen)
+        store_state(c).start()
 
         @pl.when(c >= 1)
         def _():
@@ -210,6 +288,49 @@
         return carry
 
     lax.fori_loop(0, CHUNKS, middle, 0)
+
+    def folded(g):
+        n, m = g.shape
+        return jnp.sum((g[...] * diagonal((n, m))).reshape(n // 8, 8, m), axis=1)
+
+    def lanes_of(m, first):
+        return where_equal((m, 128), lambda i: i // 8 + first, same)
+
+    def exact(a, b):
+        return jnp.dot(a, b, precision=lax.Precision.HIGHEST, preferred_element_type=F32)
+
+    pay[...] = jnp.zeros_like(pay)
+    pay[0:HIDDEN] = exact(folded(g1_ref), lanes_of(EXTENDED * 8, 0)) + exact(
+        folded(g2_ref), lanes_of(FIELDS * 8, 32)
+    )
+    out_bias = jnp.sum(g3_ref[...].reshape(FIELDS, 8, 128), axis=1)
+    pay[HIDDEN : HIDDEN + 8] = jnp.concatenate([out_bias, jnp.zeros((3, 128), F32)], axis=0)
+
+    def eight(d):
+        return pl.ds(pl.multiple_of(8 * d, 8), 8)
+
+    def small(stage, s):
+        axis, mine = (("space", me), ("dp", team), ("space", me))[stage]
+        dst = lax.rem(mine + s, GROUP)
+        source = pay.at[eight(dst)] if stage == 0 else piece.at[stage - 1]
+        return pltpu.make_async_remote_copy(
+            src_ref=source,
+            dst_ref=slots.at[stage, mine],
+            send_sem=msem.at[stage, s],
+            recv_sem=nsem.at[stage, s],
+            device_id={axis: dst},
+            device_id_type=MESH,
+        )
+
+    def begin(stage):
+        each(lambda s: small(stage, s).start())
+
+    def collect(stage):
+        each(lambda s: small(stage, s).wait())
+        return sum(slots[stage, d] for d in range(1, GROUP)) + slots[stage, 0]
+
+    slots[0, me] = pay[eight(me)]
+    begin(0)
 
     def adjoint_lines(a, carry):
         for f in range(FIELDS):
@@ -225,7 +346,15 @@
         return carry
 
     lax.fori_loop(0, GROUP, adjoint_lines, 0)
+    over_space = collect(0)
+    piece[0] = over_space
+    slots[1, team] = over_space
+    begin(1)
     backward_lines(CHUNKS - 1)
+    over_all = collect(1)
+    piece[1] = over_all
+    slots[2, me] = over_all
+    begin(2)
 
     def last(c, carry):
         finish(3, c, recv)
@@ -234,83 +363,87 @@
             back = dot(perm_ref[...], recv[c, :, :, lanes].reshape(256, PACK))
             whole = (back.reshape(16, 16, PACK) + loc[c, f]).astype(BF16)
             first, second = unpack(whole)
-            sg_ref[f, :, rows(c, 0), :] = first
-            sg_ref[f, :, rows(c, 1), :] = second
-        return carry
-
-    lax.fori_loop(0, CHUNKS, last, 0)
-
-
-def spread(w):
-    n, m = w.shape
-    eye = jnp.eye(8, dtype=w.dtype)
-    return (w[:, None, :, None] * eye[None, :, None, :]).reshape(n * 8, m * 8)
-
-
-def gather(g, n, m):
-    eye = jnp.eye(8, dtype=F32)
-    return jnp.sum(g.reshape(n, 8, m, 8) * eye[None, :, None, :], axis=(1, 3))
+            s_ref[f, :, rows(c, 0), :] = first
+            s_ref[f, :, rows(c, 1), :] = second
+        store_grad(c).start()
+        return carry
+
+    lax.fori_loop(0, CHUNKS - 1, last, 0)
+    each(lambda s: small(2, s).wait())
+    for d in range(HIDDEN // 8 + 1):
+        total_ref[8 * d : 8 * d + 8] = slots[2, d]
+    last(CHUNKS - 1, 0)
+    for c in range(CHUNKS):
+        store_state(c).wait()
+    for c in range(CHUNKS):
+        store_grad(c).wait()
 
 
 def body(state, cotangent, x_operator, y_operator, z_operator, w_in, b_in, w_out, b_out):
     shape = state.shape[1:]
-    hi = lax.reduce_precision(b_in, 8, 7)
-    mid = lax.reduce_precision(b_in - hi, 8, 7)
-    low = b_in - hi - mid
-    columns = jnp.stack([hi, mid, low], axis=1).astype(BF16)
-    w1 = spread(jnp.concatenate([w_in, columns], axis=1))
-    w1t = spread(w_in.T)
-    w2 = spread(w_out)
-    w2t = spread(w_out.T)
-    place = jnp.arange(256)
-    swapped = (place % 16) * 16 + place // 16
-    perm = (swapped[:, None] == place[None, :]).astype(BF16)
     vmem = pl.BlockSpec(memory_space=pltpu.VMEM)
+    hbm = pl.BlockSpec(memory_space=pl.ANY)
     buffer = pltpu.VMEM((CHUNKS, GROUP, GROUP, FIELDS * PACK), BF16)
     packed = pltpu.VMEM((CHUNKS, FIELDS, GROUP, GROUP, PACK), BF16)
     part = pltpu.VMEM((FIELDS, GROUP, GROUP, PACK), BF16)
-    ns, sg, g1, g2, g3 = pl.pallas_call(
+    whole = pltpu.VMEM(shape, BF16)
+    dma = pltpu.SemaphoreType.DMA
+    ns, sg, total = pl.pallas_call(
         step_kernel,
         out_shape=(
             jax.ShapeDtypeStruct(shape, BF16),
             jax.ShapeDtypeStruct(shape, BF16),
-            jax.ShapeDtypeStruct((HIDDEN * 8, EXTENDED * 8), F32),
-            jax.ShapeDtypeStruct((HIDDEN * 8, FIELDS * 8), F32),
-            jax.ShapeDtypeStruct((FIELDS * 8, 128), F32),
+            jax.ShapeDtypeStruct((HIDDEN + 8, 128), F32),
         ),
-        in_specs=[vmem] * 13 + [pl.BlockSpec(memory_space=pltpu.SMEM)],
-        out_specs=[vmem] * 5,
+        in_specs=[hbm] * 2 + [vmem] * 8 + [pl.BlockSpec(memory_space=pltpu.SMEM)],
+        out_specs=[hbm, hbm, vmem],
         scratch_shapes=[
+            whole, whole, whole,
+            pltpu.VMEM(x_operator.shape, BF16),
+            pltpu.VMEM(y_operator.shape, BF16),
+            pltpu.VMEM(z_operator.shape, BF16),
+            pltpu.VMEM((256, 256), BF16),
+            pltpu.VMEM((HIDDEN * 8, EXTENDED * 8), BF16),
+            pltpu.VMEM((CHANNELS * 8, HIDDEN * 8), BF16),
+            pltpu.VMEM((FIELDS * 8, HIDDEN * 8), BF16),
+            pltpu.VMEM((HIDDEN * 8, FIELDS * 8), BF16),
+            pltpu.VMEM((HIDDEN * 8, EXTENDED * 8), F32),
+            pltpu.VMEM((HIDDEN * 8, FIELDS * 8), F32),
+            pltpu.VMEM((FIELDS * 8, 128), F32),
+            pltpu.VMEM((128, 128), F32),
+            pltpu.VMEM((3, GROUP, 8, 128), F32),
+            pltpu.VMEM((2, 8, 128), F32),
+            dma((4, CHUNKS, GROUP)),
+            dma((4, CHUNKS, GROUP)),
+            dma((4, CHUNKS)),
+            dma((3, GROUP)),
+            dma((3, GROUP)),
+            dma((4, CHUNKS)),
             buffer, buffer, buffer, part, packed, packed, part, packed, packed,
             pltpu.VMEM((CHUNKS, FIELDS, GROUP, GROUP, PACK), F32),
-            pltpu.SemaphoreType.DMA((4, CHUNKS, GROUP)),
-            pltpu.SemaphoreType.DMA((4, CHUNKS, GROUP)),
-            pltpu.SemaphoreType.DMA((4, CHUNKS)),
         ],
         compiler_params=pltpu.CompilerParams(
             collective_id=0, has_side_effects=True, vmem_limit_bytes=60 * 1024 * 1024
         ),
-        cost_estimate=pl.CostEstimate(flops=10**11, bytes_accessed=2 * 10**7, transcendentals=2 * 10**7),
+        cost_estimate=pl.CostEstimate(
+            flops=10**11, bytes_accessed=2 * 10**7, transcendentals=2 * 10**7
+        ),
         name="evolution",
     )(
-        state[0], cotangent[0], x_operator, x_operator.T, y_operator, y_operator.T,
-        z_operator, z_operator.T, perm, w1, w1t, w2, w2t, b_out,
+        state[0], cotangent[0], x_operator, y_operator, z_operator,
+        w_in, w_in.T, b_in[:, None], w_out, w_out.T, b_out,
     )
-    w_in_all = gather(g1, HIDDEN, EXTENDED)
-    w_out_all = gather(g2, HIDDEN, FIELDS).T
-    b_out_all = jnp.sum(g3.reshape(FIELDS, 8 * 128), axis=1)
-    summed = lax.psum((w_in_all, w_out_all, b_out_all), ("dp", "space"))
     cells = (
         lax.axis_size("dp") * lax.axis_size("space") * shape[1] * shape[2] * shape[3]
     )
-    scaling = 1.0 / math.sqrt(cells)
+    scaled = total * (1.0 / math.sqrt(cells))
     return (
         ns[None],
         sg[None],
-        summed[0][:, 0:CHANNELS] * scaling,
-        summed[0][:, CHANNELS] * scaling,
-        summed[1] * scaling,
-        summed[2] * scaling,
+        scaled[0:HIDDEN, 0:CHANNELS],
+        scaled[0:HIDDEN, CHANNELS],
+        scaled[0:HIDDEN, 32 : 32 + FIELDS].T,
+        jnp.sum(scaled[HIDDEN : HIDDEN + FIELDS], axis=1),
     )
 
 

time: 403 us -> 304 us (0.75)
  blocking collectives: 80.6 us -> 0 us
  local copies, waits for them, and re-layouts: 34.8 us -> 12.8 us
  Pallas kernels: 275 us -> 289 us
  other arithmetic: 11 us -> 1.4 us
    psum x1 -> x0, blocking collectives: 80.6 us -> none  [body(): summed = lax.psum((w_in_all, w_out_all, b_out_all), ('dp', 'space'))]
    mul x6 -> x0, local copies, waits for them, and re-layouts: 14.3 us -> none  [spread(): return (w[:, None, :, None] * eye[None, :, None, :]).reshape(n * 8, m * 8)]
    pallas_call x1, Pallas kernels: 275 us -> 289 us  [body(): pl.pallas_call(step_kernel, out_shape=(jax.ShapeDtypeStruct(shape, BF16),...]
    reshape x2 -> x0, local copies, waits for them, and re-layouts: 6.81 us -> none  [gather(): return jnp.sum(g.reshape(n, 8, m, 8) * eye[None, :, None, :], axis=(1, 3))]
    unnamed x9 -> x8, local copies, waits for them, and re-layouts: 11.2 us -> 10.6 us
where the time goes in v2:
time: 304 us; the launch traced here: 303 us
  Pallas kernels  289 us (95%)
  local copies, waits for them, and re-layouts  12.8 us (4%)
    pallas_call x1, Pallas kernels, body(): pl.pallas_call(step_kernel, out_shape=(jax.ShapeDtypeStruct(shape, BF16),...  289 us
    unnamed x8, local copies, waits for them, and re-layouts  10.6 us

profile of v2, /device:TPU:1, one launch (start us, length us, event | category | flops | bytes accessed | tf_op | source)
XLA Modules:
  0.0 303.4 jit_solution(15910013218489343149)
XLA Ops:
  0.6 1.4 copy.22.b_ref
  2.0 1.4 copy.20
  3.4 1.4 copy.21.wi_ref
  4.8 288.6 %evolution.1 = (bf16[5,16,96,192]{3,2,1,0:T(8,128)(2,1)}, bf16[5,16,96,192]{3,2,1,0:T(8,128)(2,1)}, f32[72,128]{1,0:T(8,128)}) custom-call(bf16[5,16,96,192]{3,2,1,0:T(8,128)(2,1)} %bitcast.14, bf16[5,16,96,192]{3,2,1,0:T(8,128)(2,1)} %bitcast.15, bf16[256,256]{1,0:T(8,128)(2,1)} %x_ref.1, bf16[96,96]{1,0:T(8,128)(2,1)} %y_ref.1, bf16[192,192]{1,0:T(8,128)(2,1)} %z_ref.1, ...), custom_call_target="tpu_custom_call" | custom-call | flops 99999997952 | bytes 20000000 | tf_op jit(solution)/shard_map/evolution/pallas_call | solution.py:391
  293.4 0.8 broadcast_multiply_fusion
  294.1 0.7 copy.23
  294.8 0.1 slice_bitcast_fusion
  294.9 0.7 copy.24
  295.6 0.7 slice_reduce_fusion
  296.3 0.6 slice_reduce_fusion.1
  296.9 0.0 copy-start
  296.9 4.6 %copy.27 = bf16[1,5,16,96,192]{4,3,2,1,0:T(8,128)(2,1)} copy(bf16[1,5,16,96,192]{4,3,2,1,0:T(8,128)(2,1)} %bitcast.10) | data formatting | bytes 5898240
  301.5 0.0 copy-done
  301.5 1.9 copy.28
  (1 shorter events, 0.0 us)
Async XLA Ops:
  296.9 4.6 %copy-start = (bf16[5,16,96,192]{3,2,1,0:T(8,128)(2,1)S(1)}, bf16[5,16,96,192]{3,2,1,0:T(8,128)(2,1)}, u32[]{:S(2)}) copy-start(bf16[5,16,96,192]{3,2,1,0:T(8,128)(2,1)} %get-tuple-element.10) | copy-start | bytes 8847364

commit v3 on v2

--- a/solution.py
+++ b/solution.py
@@ -65,17 +65,20 @@
 
 
 def step_kernel(
-    s_hbm, c_hbm, x_ref, y_ref, z_ref, wi_ref, wit_ref, b_ref, wo_ref, wot_ref, bo_ref,
-    ns_hbm, sg_hbm, total_ref,
-    s_ref, c_ref, ns_ref, xt_ref, yt_ref, zt_ref, perm_ref, w1_ref, w1t_ref, w2_ref, w2t_ref,
+    scaling, s_hbm, c_hbm, x_ref, y_ref, z_ref, wit_ref, b_ref, wo_ref, bo_ref,
+    ns_ref, sg_ref, total_ref,
+    s_ref, c_ref, xt_ref, yt_ref, zt_ref, perm_ref, w1_ref, w1t_ref, w2_ref, w2t_ref,
     g1_ref, g2_ref, g3_ref, pay, slots, piece, ssem, rsem, lsem, msem, nsem, iosem,
     send, pen, recv, gx, gy, gz, cx, cy, cz, loc,
 ):
     me = lax.axis_index("space")
     team = lax.axis_index("dp")
 
+    def shifted(s):
+        return lax.rem(me // 4 + s % 4, 4) * 4 + lax.rem(me % 4 + s // 4, 4)
+
     def copy_of(phase, c, s, target):
-        dst = lax.rem(me + s, GROUP)
+        dst = shifted(s)
         return pltpu.make_async_remote_copy(
             src_ref=send.at[c, dst],
             dst_ref=target.at[c, me],
@@ -119,21 +122,8 @@
             c_hbm.at[:, :, chunk(c), :], c_ref.at[:, :, chunk(c), :], iosem.at[1, c]
         )
 
-    def store_state(c):
-        return pltpu.make_async_copy(
-            ns_ref.at[:, :, chunk(c), :], ns_hbm.at[:, :, chunk(c), :], iosem.at[2, c]
-        )
-
-    def store_grad(c):
-        return pltpu.make_async_copy(
-            s_ref.at[:, :, chunk(c), :], sg_hbm.at[:, :, chunk(c), :], iosem.at[3, c]
-        )
-
     for c in range(CHUNKS):
         load_state(c).start()
-    for c in range(CHUNKS):
-        load_cotangent(c).start()
-
     barrier = pltpu.get_barrier_semaphore()
     for axis, mine in (("space", me), ("dp", team)):
 
@@ -159,6 +149,8 @@
         return carry
 
     lax.fori_loop(0, CHUNKS, send_state, 0)
+    for c in range(CHUNKS):
+        load_cotangent(c).start()
 
     for source, target in ((x_ref, xt_ref), (y_ref, yt_ref), (z_ref, zt_ref)):
         unit = where_equal(source.shape, same, same).astype(BF16)
@@ -173,13 +165,18 @@
     def diagonal(shape):
         return where_equal(shape, lambda i: i % 8, lambda i: i % 8)
 
-    bias = b_ref[...]
+    def turned(w):
+        unit = where_equal((w.shape[1], w.shape[1]), same, same).astype(BF16)
+        return dot_t(unit, w).astype(BF16)
+
+    unit = where_equal((HIDDEN, HIDDEN), same, same)
+    bias = jnp.sum(unit * b_ref[...], axis=1, keepdims=True)
     high = bias.astype(BF16).astype(F32)
     mid = (bias - high).astype(BF16).astype(F32)
     low = bias - high - mid
     places = iota((HIDDEN, EXTENDED * 8), 1) // 8
     right = where_equal((CHANNELS, EXTENDED * 8), same, eighth).astype(BF16)
-    inner = dot(wi_ref[...], right)
+    inner = dot(turned(wit_ref[...]), right)
     for place, column in enumerate((high, mid, low)):
         inner += jnp.where(places == CHANNELS + place, column, 0.0)
     left = where_equal((HIDDEN * 8, HIDDEN), eighth, same).astype(BF16)
@@ -187,7 +184,7 @@
     w1_ref[...] = w1.astype(BF16)
     w1t_ref[...] = spread(wit_ref[...]).astype(BF16)
     w2_ref[...] = spread(wo_ref[...]).astype(BF16)
-    w2t_ref[...] = spread(wot_ref[...]).astype(BF16)
+    w2t_ref[...] = spread(turned(wo_ref[...])).astype(BF16)
 
     def lines(a, carry):
         for f in range(FIELDS):
@@ -279,7 +276,6 @@
             moved = dot(perm_ref[...], cx[f].reshape(256, PACK)).astype(BF16)
             send[c, :, :, lanes] = moved.reshape(16, 16, PACK)
         start(2, c, pen)
-        store_state(c).start()
 
         @pl.when(c >= 1)
         def _():
@@ -293,18 +289,17 @@
         n, m = g.shape
         return jnp.sum((g[...] * diagonal((n, m))).reshape(n // 8, 8, m), axis=1)
 
-    def lanes_of(m, first):
-        return where_equal((m, 128), lambda i: i // 8 + first, same)
-
-    def exact(a, b):
-        return jnp.dot(a, b, precision=lax.Precision.HIGHEST, preferred_element_type=F32)
+    def summed(g, first):
+        select = where_equal((40, g.shape[1]), same, lambda i: i // 8 + first)
+        return lax.dot_general(
+            select, folded(g), (((1,), (1,)), ((), ())),
+            precision=lax.Precision.HIGHEST, preferred_element_type=F32,
+        )
 
     pay[...] = jnp.zeros_like(pay)
-    pay[0:HIDDEN] = exact(folded(g1_ref), lanes_of(EXTENDED * 8, 0)) + exact(
-        folded(g2_ref), lanes_of(FIELDS * 8, 32)
-    )
+    pay[0:40, 0:HIDDEN] = summed(g1_ref, 0) + summed(g2_ref, 32)
     out_bias = jnp.sum(g3_ref[...].reshape(FIELDS, 8, 128), axis=1)
-    pay[HIDDEN : HIDDEN + 8] = jnp.concatenate([out_bias, jnp.zeros((3, 128), F32)], axis=0)
+    pay[40:48] = jnp.concatenate([out_bias, jnp.zeros((3, 128), F32)], axis=0)
 
     def eight(d):
         return pl.ds(pl.multiple_of(8 * d, 8), 8)
@@ -351,7 +346,7 @@
     slots[1, team] = over_space
     begin(1)
     backward_lines(CHUNKS - 1)
-    over_all = collect(1)
+    over_all = collect(1) * scaling
     piece[1] = over_all
     slots[2, me] = over_all
     begin(2)
@@ -363,20 +358,15 @@
             back = dot(perm_ref[...], recv[c, :, :, lanes].reshape(256, PACK))
             whole = (back.reshape(16, 16, PACK) + loc[c, f]).astype(BF16)
             first, second = unpack(whole)
-            s_ref[f, :, rows(c, 0), :] = first
-            s_ref[f, :, rows(c, 1), :] = second
-        store_grad(c).start()
+            sg_ref[f, :, rows(c, 0), :] = first
+            sg_ref[f, :, rows(c, 1), :] = second
         return carry
 
     lax.fori_loop(0, CHUNKS - 1, last, 0)
     each(lambda s: small(2, s).wait())
-    for d in range(HIDDEN // 8 + 1):
+    for d in range(6):
         total_ref[8 * d : 8 * d + 8] = slots[2, d]
     last(CHUNKS - 1, 0)
-    for c in range(CHUNKS):
-        store_state(c).wait()
-    for c in range(CHUNKS):
-        store_grad(c).wait()
 
 
 def body(state, cotangent, x_operator, y_operator, z_operator, w_in, b_in, w_out, b_out):
@@ -388,17 +378,20 @@
     part = pltpu.VMEM((FIELDS, GROUP, GROUP, PACK), BF16)
     whole = pltpu.VMEM(shape, BF16)
     dma = pltpu.SemaphoreType.DMA
+    cells = (
+        lax.axis_size("dp") * lax.axis_size("space") * shape[1] * shape[2] * shape[3]
+    )
     ns, sg, total = pl.pallas_call(
-        step_kernel,
+        functools.partial(step_kernel, 1.0 / math.sqrt(cells)),
         out_shape=(
-            jax.ShapeDtypeStruct(shape, BF16),
-            jax.ShapeDtypeStruct(shape, BF16),
-            jax.ShapeDtypeStruct((HIDDEN + 8, 128), F32),
+            pltpu.VMEM(shape, BF16),
+            pltpu.VMEM(shape, BF16),
+            jax.ShapeDtypeStruct((48, 128), F32),
         ),
-        in_specs=[hbm] * 2 + [vmem] * 8 + [pl.BlockSpec(memory_space=pltpu.SMEM)],
-        out_specs=[hbm, hbm, vmem],
+        in_specs=[hbm] * 2 + [vmem] * 6 + [pl.BlockSpec(memory_space=pltpu.SMEM)],
+        out_specs=[vmem] * 3,
         scratch_shapes=[
-            whole, whole, whole,
+            whole, whole,
             pltpu.VMEM(x_operator.shape, BF16),
             pltpu.VMEM(y_operator.shape, BF16),
             pltpu.VMEM(z_operator.shape, BF16),
@@ -418,12 +411,12 @@
             dma((4, CHUNKS)),
             dma((3, GROUP)),
             dma((3, GROUP)),
-            dma((4, CHUNKS)),
+            dma((2, CHUNKS)),
             buffer, buffer, buffer, part, packed, packed, part, packed, packed,
             pltpu.VMEM((CHUNKS, FIELDS, GROUP, GROUP, PACK), F32),
         ],
         compiler_params=pltpu.CompilerParams(
-            collective_id=0, has_side_effects=True, vmem_limit_bytes=60 * 1024 * 1024
+            collective_id=0, has_side_effects=True, vmem_limit_bytes=52 * 1024 * 1024
         ),
         cost_estimate=pl.CostEstimate(
             flops=10**11, bytes_accessed=2 * 10**7, transcendentals=2 * 10**7
@@ -431,19 +424,15 @@
         name="evolution",
     )(
         state[0], cotangent[0], x_operator, y_operator, z_operator,
-        w_in, w_in.T, b_in[:, None], w_out, w_out.T, b_out,
+        w_in.T, b_in[None, :], w_out, b_out,
     )
-    cells = (
-        lax.axis_size("dp") * lax.axis_size("space") * shape[1] * shape[2] * shape[3]
-    )
-    scaled = total * (1.0 / math.sqrt(cells))
     return (
         ns[None],
         sg[None],
-        scaled[0:HIDDEN, 0:CHANNELS],
-        scaled[0:HIDDEN, CHANNELS],
-        scaled[0:HIDDEN, 32 : 32 + FIELDS].T,
-        jnp.sum(scaled[HIDDEN : HIDDEN + FIELDS], axis=1),
+        total[0:CHANNELS, 0:HIDDEN].T,
+        total[CHANNELS, 0:HIDDEN],
+        total[32 : 32 + FIELDS, 0:HIDDEN],
+        jnp.sum(total[40 : 40 + FIELDS], axis=1),
     )
 
 

time: 304 us -> 297 us (0.977)
  local copies, waits for them, and re-layouts: 12.8 us -> 7.6 us
    unnamed x8 -> x2, local copies, waits for them, and re-layouts: 10.6 us -> 3.84 us
where the time goes in v3:
time: 297 us
  Pallas kernels  287 us (97%)
  local copies, waits for them, and re-layouts  7.6 us (3%)
    pallas_call x1, Pallas kernels, body(): pl.pallas_call(functools.partial(step_kernel, 1.0 / math.sqrt(cells)), ou...  287 us

profile of v3, /device:TPU:1, one launch (start us, length us, event | category | flops | bytes accessed | tf_op | source)
XLA Modules:
  0.0 296.8 jit_solution(4185116569535992130)
XLA Ops:
  0.6 287.3 %evolution.1 = (bf16[5,16,96,192]{3,2,1,0:T(8,128)(2,1)S(1)}, bf16[5,16,96,192]{3,2,1,0:T(8,128)(2,1)S(1)}, f32[48,128]{1,0:T(8,128)}) custom-call(bf16[5,16,96,192]{3,2,1,0:T(8,128)(2,1)} %bitcast.12, bf16[5,16,96,192]{3,2,1,0:T(8,128)(2,1)} %bitcast.13, bf16[256,256]{1,0:T(8,128)(2,1)} %x_ref.1, bf16[96,96]{1,0:T(8,128)(2,1)} %y_ref.1, ...), custom_call_target="tpu_custom_call" | custom-call | flops 99999997952 | bytes 20000000 | tf_op jit(solution)/shard_map/evolution/pallas_call | solution.py:384
  287.9 1.3 slice_bitcast_fusion
  289.2 1.3 slice.14
  290.5 1.2 slice_bitcast_fusion.1
  291.7 1.3 slice_reduce_fusion
  293.0 1.9 copy.17
  294.9 1.9 copy.18

commit v4 on v3

--- a/solution.py
+++ b/solution.py
@@ -136,19 +136,24 @@
     perm_ref[...] = where_equal(
         (256, 256), lambda i: (i % 16) * 16 + i // 16, same
     ).astype(BF16)
-    pl.semaphore_wait(barrier, 2 * (GROUP - 1))
-
-    def send_state(c, carry):
+
+    def pack_state(c):
         load_state(c).wait()
         for f in range(FIELDS):
             a = s_ref[f, :, rows(c, 0), :].reshape(256, 192)
             b = s_ref[f, :, rows(c, 1), :].reshape(256, 192)
             moved = dot(perm_ref[...], pack(a, b)).astype(BF16)
             send[c, :, :, f * PACK : (f + 1) * PACK] = moved.reshape(16, 16, PACK)
+
+    def send_state(c, carry):
+        pack_state(c)
         start(0, c, pen)
         return carry
 
-    lax.fori_loop(0, CHUNKS, send_state, 0)
+    pack_state(0)
+    pl.semaphore_wait(barrier, 2 * (GROUP - 1))
+    start(0, 0, pen)
+    lax.fori_loop(1, CHUNKS, send_state, 0)
     for c in range(CHUNKS):
         load_cotangent(c).start()
 
@@ -386,7 +391,7 @@
         out_shape=(
             pltpu.VMEM(shape, BF16),
             pltpu.VMEM(shape, BF16),
-            jax.ShapeDtypeStruct((48, 128), F32),
+            pltpu.VMEM((48, 128), F32),
         ),
         in_specs=[hbm] * 2 + [vmem] * 6 + [pl.BlockSpec(memory_space=pltpu.SMEM)],
         out_specs=[vmem] * 3,

time: 297 us -> 294 us (0.990)
  no operation moved by 1% of the time
where the time goes in v4:
time: 294 us; the launch traced here: 293 us
  Pallas kernels  287 us (98%)
  local copies, waits for them, and re-layouts  5.55 us (2%)
    pallas_call x1, Pallas kernels, body(): pl.pallas_call(functools.partial(step_kernel, 1.0 / math.sqrt(cells)), ou...  287 us

profile of v4, /device:TPU:1, one launch (start us, length us, event | category | flops | bytes accessed | tf_op | source)
XLA Modules:
  0.0 293.5 jit_solution(17442600165518166807)
XLA Ops:
  0.6 286.7 %evolution.1 = (bf16[5,16,96,192]{3,2,1,0:T(8,128)(2,1)S(1)}, bf16[5,16,96,192]{3,2,1,0:T(8,128)(2,1)S(1)}, f32[48,128]{1,0:T(8,128)S(1)}) custom-call(bf16[5,16,96,192]{3,2,1,0:T(8,128)(2,1)} %bitcast.12, bf16[5,16,96,192]{3,2,1,0:T(8,128)(2,1)} %bitcast.13, bf16[256,256]{1,0:T(8,128)(2,1)} %x_ref.1, bf16[96,96]{1,0:T(8,128)(2,1)} %y_ref.1, ...), custom_call_target="tpu_custom_call" | custom-call | flops 99999997952 | bytes 20000000 | tf_op jit(solution)/shard_map/evolution/pallas_call | solution.py:389
  287.3 0.6 slice_bitcast_fusion
  287.9 0.6 slice.14
  288.5 0.5 slice_bitcast_fusion.1
  289.0 0.6 slice_reduce_fusion
  289.6 1.9 copy.17
  291.6 1.9 copy.18
